TPU v7x, 32 devices: a whole 2x2x4 slice. The times are simulated.
32 devices in a mesh: groups: 2 (over x), clus: 16 (over z, y, core).
Axes of the slice: x: 2, y: 2, z: 4, core: 2. Of those that a mesh axis runs over, the one named last changes fastest.
Arguments:
- mesh_current: float32 [2, 131072], P(None, ('groups', 'clus')), parts along dimension 1, may hold values from -6 to 6
- branch_entry: int32 [2, 262144], P(None, ('groups', 'clus')), parts along dimension 1, may hold values from 0 to 6143, as said below
- branch_sign: int32 [2, 262144], P(None, ('groups', 'clus')), parts along dimension 1, may hold values from 0 to 1
- need_slots: int32 [512, 128], P(('groups', 'clus')), parts along dimension 0, may hold values from -1 to 4095, as said below
- resistance: float32 [262144], P(('groups', 'clus')), parts along dimension 0, may hold values from 0.3 to 3
- near_blocks: bfloat16 [2048, 4, 128, 128], P(('groups', 'clus')), parts along dimension 0, may hold values from -0.25 to 0.25
- near_source: int32 [2048, 4], P(('groups', 'clus')), parts along dimension 0, may hold values from 0 to 63
- basis_in: bfloat16 [2048, 32, 128], P(('groups', 'clus')), parts along dimension 0, may hold values from -0.5 to 0.5
- coupling: bfloat16 [2048, 16, 32, 32], P(('groups', 'clus')), parts along dimension 0, may hold values from -0.25 to 0.25
- basis_out: bfloat16 [2048, 32, 128], P(('groups', 'clus')), parts along dimension 0, may hold values from -1 to 1
- admissible: int32 [2048, 16], P(('groups', 'clus')), parts along dimension 0, may hold values from 0 to 1023, as said below
- port_mesh: int32 [128], P('groups'), parts along dimension 0, may hold values from 0 to 65535, as said below
- port_coupling: float32 [2, 64, 64], replicated, may hold values from -0.75 to 0.75
Outputs:
- mesh_voltage: float32 [2, 131072], P(None, ('groups', 'clus')), parts along dimension 1
There are 2 independent parts, one for each index of `groups`. A program takes and returns all parts, laid end to end along the dimension named above; an argument that names none is the same for every part. Nothing has to cross between parts.
Inputs may be any that keep to these rules, and one draw needn't show every extreme that they name: `need_slots`: row d * 16 + p holds distinct meshes of device p, counted from 0 within it, in its first slots and -1 in the rest. Row d * 16 + d is all -1; row d * 16 + (d + 1) % 16 has no -1. `branch_entry`: A value below 4096 is a mesh of the branch's own device d. Any other value is 4096 + p * 128 + s with p != d and slot s of row d * 16 + p of need_slots not -1. `admissible`: entry k of row t is (t + k * 64 + o) % 1024 with 1 <= o < 64; the entries of a row are distinct and never t. `port_mesh`: distinct meshes.
All inputs are finite; a program needn't handle non-finite values.
Results may differ from a plain program's by a relative error of at most 0.0021.
Values may be sent and summed in bfloat16 or wider, within the bound.
A program may use at most 320 MiB of HBM per device.

v0:
```python
import functools

import jax
import jax.numpy as jnp
from jax import lax
from jax.experimental import pallas as pl
from jax.experimental.pallas import tpu as pltpu
from jax.sharding import PartitionSpec as P

LANES = 128
CHUNK = 1024
VMEM_LIMIT = 48 * 1024 * 1024
NT = (((1,), (1,)), ((), ()))


def greet(peers):
    me = lax.axis_index("clus")
    barrier = pltpu.get_barrier_semaphore()

    @pl.loop(1, peers)
    def _(step):
        pl.semaphore_signal(
            barrier,
            inc=1,
            device_id={"clus": lax.rem(me + step, peers)},
            device_id_type=pl.DeviceIdType.MESH,
        )

    pl.semaphore_wait(barrier, peers - 1)


def push(peers, phase, x_ref, o_ref, send_sem, recv_sem, own_sem, gather=False):
    me = lax.axis_index("clus")

    def copy_at(step):
        peer = lax.rem(me + step, peers)
        return pltpu.make_async_remote_copy(
            src_ref=x_ref if gather else x_ref.at[peer],
            dst_ref=o_ref.at[me],
            send_sem=send_sem.at[phase, step],
            recv_sem=recv_sem.at[phase, step],
            device_id={"clus": peer},
            device_id_type=pl.DeviceIdType.MESH,
        )

    @pl.loop(1, peers)
    def _(step):
        copy_at(step).start()

    own = pltpu.make_async_copy(x_ref if gather else x_ref.at[me], o_ref.at[me], own_sem.at[phase])
    own.start()

    def finish():
        own.wait()

        @pl.loop(1, peers)
        def _(step):
            copy_at(step).wait()

    return finish


def near_work(flow_ref, source_ref, blocks_ref, near_ref, picked_ref):
    tile_dev, near_count = blocks_ref.shape[:2]
    count = source_ref.shape[0]
    hot = jnp.where(
        lax.broadcasted_iota(jnp.int32, (count, tile_dev), 1) == source_ref[...], 1.0, 0.0
    ).astype(jnp.bfloat16)
    for c in range(2):
        picked_ref[c] = jnp.dot(
            hot, flow_ref[c].astype(jnp.bfloat16), preferred_element_type=jnp.float32
        )

    @pl.loop(0, tile_dev // 8)
    def _(step):
        rows = []
        for j in range(8):
            tile = step * 8 + j
            total = 0.0
            for k in range(near_count):
                place = pl.ds(tile * near_count + k, 1)
                source = jnp.concatenate([picked_ref[0, place, :], picked_ref[1, place, :]], axis=0)
                total += lax.dot_general(
                    source.astype(jnp.bfloat16),
                    blocks_ref[tile, k],
                    NT,
                    preferred_element_type=jnp.float32,
                )
            rows.append(total)
        for c in range(2):
            near_ref[c, pl.ds(pl.multiple_of(step * 8, 8), 8), :] = jnp.concatenate(
                [row[c : c + 1] for row in rows], axis=0
            )


def split(value):
    high = value.astype(jnp.bfloat16).astype(jnp.float32)
    return high, value - high


def lanes_one_hot(index):
    low = index & (LANES - 1)
    rows = lax.broadcasted_iota(jnp.int32, (LANES, index.shape[1]), 0)
    return jnp.where(rows == low, 1.0, 0.0).astype(jnp.bfloat16)


def rows_mask(index, rows):
    return lax.broadcasted_iota(jnp.int32, (rows, index.shape[1]), 0) == (index >> 7)


def lookup_operand(tables):
    high, low = split(jnp.concatenate(tables, axis=0))
    return jnp.concatenate([high.astype(jnp.bfloat16), low.astype(jnp.bfloat16)], axis=1)


def look_up(operand, index, rows):
    hot = lanes_one_hot(index)
    found = jnp.dot(
        operand, jnp.concatenate([hot, hot], axis=0), preferred_element_type=jnp.float32
    )
    mask = rows_mask(index, rows)
    return [
        jnp.sum(jnp.where(mask, found[c * rows : (c + 1) * rows], 0.0), axis=0, keepdims=True)
        for c in range(2)
    ]


def sums(values, index, rows):
    hot = lanes_one_hot(index)
    mask = rows_mask(index, rows)
    parts = [split(value) for value in values]
    spread = [
        jnp.where(mask, parts[c][part], 0.0).astype(jnp.bfloat16)
        for part in range(2)
        for c in range(2)
    ]
    made = lax.dot_general(
        jnp.concatenate(spread, axis=0), hot, NT, preferred_element_type=jnp.float32
    )
    return made[: 2 * rows] + made[2 * rows :]


def row_of(ref, row, peers):
    return jnp.concatenate([ref[p, row : row + 1, :] for p in range(peers)], axis=1)


def answer_kernel(peers, mesh_rows, current_ref, asked_ref, port_ref, o_ref):
    operand = lookup_operand([current_ref[0], current_ref[1]])
    o_ref[...] = jnp.zeros_like(o_ref)
    asked = look_up(operand, row_of(asked_ref, 0, peers), mesh_rows)
    ports = look_up(operand, port_ref[...], mesh_rows)
    for p in range(peers):
        for c in range(2):
            o_ref[p, c : c + 1, :] = asked[c][:, p * LANES : (p + 1) * LANES]
            o_ref[p, 2 + c : 3 + c, :] = ports[c]


def branch_kernel(
    peers, rows, current_ref, remote_ref, entry_ref, sign_ref, basis_ref, flow_ref, coeff_ref
):
    operand = lookup_operand(
        [
            part
            for c in range(2)
            for part in [current_ref[c]] + [remote_ref[p, c : c + 1, :] for p in range(peers)]
        ]
    )

    @pl.loop(0, entry_ref.shape[1] // CHUNK)
    def _(step):
        columns = pl.ds(pl.multiple_of(step * CHUNK, CHUNK), CHUNK)
        total = [0.0, 0.0]
        for k in range(entry_ref.shape[0]):
            orient = (2 * sign_ref[k : k + 1, columns] - 1).astype(jnp.float32)
            found = look_up(operand, entry_ref[k : k + 1, columns], rows)
            total = [total[c] + orient * found[c] for c in range(2)]
        tiles = CHUNK // LANES
        for c in range(2):
            flow_ref[c, pl.ds(pl.multiple_of(step * tiles, tiles), tiles), :] = jnp.concatenate(
                [total[c][:, j * LANES : (j + 1) * LANES] for j in range(tiles)], axis=0
            )

    tile_dev = flow_ref.shape[1]
    rank = basis_ref.shape[0] // tile_dev
    flows = jnp.concatenate([flow_ref[0], flow_ref[1]], axis=0).astype(jnp.bfloat16)
    part = 8
    total = jnp.zeros((rank, 2 * tile_dev), jnp.float32)
    for start in range(0, tile_dev, part):
        crossed = lax.dot_general(
            basis_ref[start * rank : (start + part) * rank, :],
            flows,
            NT,
            preferred_element_type=jnp.float32,
        )
        lane = lax.broadcasted_iota(jnp.int32, (rank, 2 * tile_dev), 1) & (tile_dev - 1)
        for j in range(part):
            total += jnp.where(lane == start + j, crossed[j * rank : (j + 1) * rank], 0.0)
    coeff_ref[...] = total.astype(jnp.bfloat16)


def far_and_collect_kernel(
    peers,
    rows,
    coeff_ref,
    admissible_ref,
    coupling_ref,
    basis_ref,
    near_ref,
    flow_ref,
    resistance_ref,
    entry_ref,
    sign_ref,
    o_ref,
    picked_ref,
    mixed_ref,
    voltage_ref,
):
    tile_dev, rank = basis_ref.shape[:2]
    far_count = coupling_ref.shape[0]
    group = 8
    held = coeff_ref[...].reshape(peers * rank, 2 * tile_dev)
    for start in range(0, admissible_ref.shape[1], 512):
        index = admissible_ref[:, start : start + 512]
        low = index & (tile_dev - 1)
        owner = index // tile_dev
        lane = lax.broadcasted_iota(jnp.int32, (1, 512), 1)
        place = low + (lane & tile_dev)
        tile = lax.broadcasted_iota(jnp.int32, (2 * tile_dev, 512), 0)
        hot = jnp.where(tile == place, 1.0, 0.0).astype(jnp.bfloat16)
        found = jnp.dot(held, hot, preferred_element_type=jnp.float32)
        total = jnp.zeros((rank, 512), jnp.float32)
        for p in range(peers):
            total += jnp.where(owner == p, found[p * rank : (p + 1) * rank], 0.0)
        for j in range(512 // LANES):
            for c in range(2):
                half = j * LANES + c * tile_dev
                picked_ref[c, start // LANES + j, :, :tile_dev] = total[:, half : half + tile_dev]
    mixed_ref[...] = jnp.zeros_like(mixed_ref)

    @pl.loop(0, rank)
    def _(r):
        total = [0.0, 0.0]
        for k in range(far_count):
            block = coupling_ref[k, r].astype(jnp.float32)
            total = [total[c] + block * picked_ref[c, k, :, :tile_dev] for c in range(2)]
        for c in range(2):
            mixed_ref[pl.ds(c * rank + r, 1), :tile_dev] = jnp.sum(
                total[c], axis=0, keepdims=True
            )

    @pl.loop(0, tile_dev // group)
    def _(step):
        spread = jnp.where(
            lax.broadcasted_iota(jnp.int32, (2 * LANES, group * LANES), 0) % LANES - step * group
            == lax.broadcasted_iota(jnp.int32, (2 * LANES, group * LANES), 1) // LANES,
            1.0,
            0.0,
        ).astype(jnp.bfloat16)
        far = []
        for c in range(2):
            wide = jnp.dot(
                lookup_operand([mixed_ref[c * rank : (c + 1) * rank, :]]),
                spread,
                preferred_element_type=jnp.float32,
            )
            wide = wide.astype(jnp.bfloat16).astype(jnp.float32)
            far.append(
                jnp.concatenate(
                    [
                        jnp.sum(
                            basis_ref[step * group + j].astype(jnp.float32)
                            * wide[:, j * LANES : (j + 1) * LANES],
                            axis=0,
                            keepdims=True,
                        )
                        for j in range(group)
                    ],
                    axis=0,
                )
            )
        place = pl.ds(pl.multiple_of(step * group, group), group)
        resistance = resistance_ref[place, :]
        reactive = [near_ref[c, place, :] + far[c] for c in range(2)]
        voltage_ref[0, place, :] = resistance * flow_ref[0, place, :] - reactive[1]
        voltage_ref[1, place, :] = resistance * flow_ref[1, place, :] + reactive[0]

    o_ref[...] = jnp.zeros_like(o_ref)

    @pl.loop(0, entry_ref.shape[1] // CHUNK)
    def _(step):
        columns = pl.ds(pl.multiple_of(step * CHUNK, CHUNK), CHUNK)
        tiles = CHUNK // LANES
        voltage = [
            voltage_ref[c, pl.ds(pl.multiple_of(step * tiles, tiles), tiles), :] for c in range(2)
        ]
        voltage = [
            jnp.concatenate([value[j : j + 1] for j in range(tiles)], axis=1) for value in voltage
        ]
        for k in range(entry_ref.shape[0]):
            orient = (2 * sign_ref[k : k + 1, columns] - 1).astype(jnp.float32)
            values = [orient * voltage[c] for c in range(2)]
            o_ref[...] += sums(values, entry_ref[k : k + 1, columns], rows)


def finish_kernel(
    peers, rows, mesh_rows, sums_ref, arrived_ref, asked_ref, answer_ref, port_ref, z_ref, o_ref
):
    asked = row_of(asked_ref, 0, peers)
    arrived = sums([row_of(arrived_ref, c, peers) for c in range(2)], asked, mesh_rows)
    current = answer_ref[0]
    for p in range(1, peers):
        current = current + answer_ref[p]
    products = [
        lax.dot_general(
            current,
            z_ref[part],
            NT,
            precision=lax.Precision.HIGHEST,
            preferred_element_type=jnp.float32,
        )
        for part in range(2)
    ]
    real_part = products[0][2:3] - products[1][3:4]
    imag_part = products[0][3:4] + products[1][2:3]
    ports = sums([real_part, imag_part], port_ref[...], mesh_rows)
    for c in range(2):
        own = slice(c * mesh_rows, (c + 1) * mesh_rows)
        o_ref[c] = sums_ref[c * rows : c * rows + mesh_rows, :] + arrived[own] + ports[own]


def whole_kernel(
    peers,
    rows,
    mesh_rows,
    need_ref,
    current_ref,
    port_ref,
    entry_ref,
    sign_ref,
    basis_in_ref,
    source_ref,
    blocks_hbm,
    admissible_ref,
    coupling_hbm,
    basis_out_ref,
    resistance_ref,
    z_ref,
    o_ref,
    asked_ref,
    reply_ref,
    answer_ref,
    flow_ref,
    coeff_ref,
    all_coeff_ref,
    blocks_ref,
    coupling_ref,
    near_ref,
    near_picked_ref,
    picked_ref,
    mixed_ref,
    voltage_ref,
    totals_ref,
    slots_ref,
    arrived_ref,
    send_sem,
    recv_sem,
    own_sem,
    load_sem,
):
    load_blocks = pltpu.make_async_copy(blocks_hbm, blocks_ref, load_sem.at[0])
    load_coupling = pltpu.make_async_copy(coupling_hbm, coupling_ref, load_sem.at[1])
    load_blocks.start()
    load_coupling.start()
    sems = (send_sem, recv_sem, own_sem)
    greet(peers)
    push(peers, 0, need_ref, asked_ref, *sems)()
    answer_kernel(peers, mesh_rows, current_ref, asked_ref, port_ref, reply_ref)
    push(peers, 1, reply_ref, answer_ref, *sems)()
    branch_kernel(
        peers, rows, current_ref, answer_ref, entry_ref, sign_ref, basis_in_ref, flow_ref, coeff_ref
    )
    finish = push(peers, 2, coeff_ref, all_coeff_ref, *sems, gather=True)
    load_blocks.wait()
    near_work(flow_ref, source_ref, blocks_ref, near_ref, near_picked_ref)
    load_coupling.wait()
    finish()
    far_and_collect_kernel(
        peers,
        rows,
        all_coeff_ref,
        admissible_ref,
        coupling_ref,
        basis_out_ref,
        near_ref,
        flow_ref,
        resistance_ref,
        entry_ref,
        sign_ref,
        totals_ref,
        picked_ref,
        mixed_ref,
        voltage_ref,
    )
    for p in range(peers):
        for c in range(2):
            row = c * rows + mesh_rows + p
            slots_ref[p, c : c + 1, :] = totals_ref[row : row + 1, :]
    push(peers, 3, slots_ref, arrived_ref, *sems)()
    finish_kernel(
        peers,
        rows,
        mesh_rows,
        totals_ref,
        arrived_ref,
        asked_ref,
        answer_ref,
        port_ref,
        z_ref,
        o_ref,
    )


def f32(*shape):
    return jax.ShapeDtypeStruct(shape, jnp.float32)


def per_device(
    mesh_current,
    branch_entry,
    branch_sign,
    need_slots,
    resistance,
    near_blocks,
    near_source,
    basis_in,
    coupling,
    basis_out,
    admissible,
    port_mesh,
    port_coupling,
):
    peers = lax.axis_size("clus")
    mesh_dev = mesh_current.shape[1]
    tile_dev, near_count, tile_width = near_blocks.shape[:3]
    rank = basis_in.shape[1]
    ports = port_mesh.shape[0]
    mesh_rows = mesh_dev // LANES
    rows = mesh_rows + peers
    current = mesh_current.reshape(2, mesh_rows, LANES)
    offset = lax.axis_index("clus") * mesh_dev
    port_position = jnp.pad(port_mesh, (0, LANES - ports), constant_values=-1)[None, :] - offset
    impedance = jnp.pad(port_coupling, ((0, 0), (0, LANES - ports), (0, LANES - ports)))

    far_count = admissible.shape[1]
    vmem, hbm = pl.BlockSpec(memory_space=pltpu.VMEM), pl.BlockSpec(memory_space=pl.ANY)
    mixing = coupling.transpose(1, 2, 3, 0)
    message = pltpu.VMEM((peers, 2, LANES), jnp.float32)
    tiles = pltpu.VMEM((2, tile_dev, LANES), jnp.float32)
    made = pl.pallas_call(
        functools.partial(whole_kernel, peers, rows, mesh_rows),
        out_shape=f32(2, mesh_rows, LANES),
        in_specs=[vmem] * 7 + [hbm, vmem, hbm] + [vmem] * 3,
        out_specs=vmem,
        scratch_shapes=[
            pltpu.VMEM((peers, 1, LANES), jnp.int32),
            pltpu.VMEM((peers, 4, LANES), jnp.float32),
            pltpu.VMEM((peers, 4, LANES), jnp.float32),
            tiles,
            pltpu.VMEM((rank, 2 * tile_dev), jnp.bfloat16),
            pltpu.VMEM((peers, rank, 2 * tile_dev), jnp.bfloat16),
            pltpu.VMEM(near_blocks.shape, near_blocks.dtype),
            pltpu.VMEM(mixing.shape, mixing.dtype),
            tiles,
            pltpu.VMEM((2, tile_dev * near_count, LANES), jnp.float32),
            pltpu.VMEM((2, far_count, rank, LANES), jnp.float32),
            pltpu.VMEM((2 * rank, LANES), jnp.float32),
            tiles,
            pltpu.VMEM((2 * rows, LANES), jnp.float32),
            message,
            message,
            pltpu.SemaphoreType.DMA((4, peers)),
            pltpu.SemaphoreType.DMA((4, peers)),
            pltpu.SemaphoreType.DMA((4,)),
            pltpu.SemaphoreType.DMA((2,)),
        ],
        compiler_params=pltpu.CompilerParams(
            collective_id=0, has_side_effects=True, vmem_limit_bytes=VMEM_LIMIT
        ),
    )(
        need_slots[:, None, :],
        current,
        port_position,
        branch_entry,
        branch_sign,
        basis_in.reshape(tile_dev * rank, tile_width),
        near_source.reshape(-1, 1),
        near_blocks,
        jnp.concatenate([admissible.T, admissible.T], axis=1).reshape(1, -1),
        mixing,
        basis_out,
        resistance.reshape(tile_dev, tile_width),
        impedance,
    )
    return made.reshape(2, mesh_dev)


def solution(mesh):
    in_specs = (
        P(None, ("groups", "clus")),
        P(None, ("groups", "clus")),
        P(None, ("groups", "clus")),
        P(("groups", "clus"), None),
        P(("groups", "clus")),
        P(("groups", "clus"), None, None, None),
        P(("groups", "clus"), None),
        P(("groups", "clus"), None, None),
        P(("groups", "clus"), None, None, None),
        P(("groups", "clus"), None, None),
        P(("groups", "clus"), None),
        P("groups"),
        P(),
    )
    out_specs = P(None, ("groups", "clus"))
    return jax.shard_map(
        per_device, mesh=mesh, in_specs=in_specs, out_specs=out_specs, check_vma=False
    )
```

profile of v0, /device:TPU:0, one launch (start us, length us, event | category | flops | bytes accessed | tf_op | source)
XLA Modules:
  0.0 49.7 jit_solution(979930710546400120)
XLA Ops:
  0.0 0.7 %subtract_bitcast_fusion.port_ref = s32[1,128]{1,0:T(1,128)S(1)} fusion(s32[64]{0:T(128)} %param.24, s32[]{:T(128)S(6)} %mul.3), kind=kLoop, calls=%fused_computation.3 | loop fusion | flops 128 | bytes 772 | tf_op jit(solution)/shard_map/sub | solution.py:451
  0.7 0.8 %pad_add_fusion = s32[16,128]{1,0:T(8,128)S(1)} fusion(s32[16,64]{1,0:T(8,128)} %bitcast.24), kind=kLoop, calls=%fused_computation.2 | loop fusion | flops 2048 | bytes 12288 | tf_op jit(solution)/shard_map/concatenate | solution.py:498
  1.5 0.8 %copy.22 = f32[1,2,32,128]{3,2,1,0:T(8,128)S(1)} copy(f32[1,2,32,128]{3,1,2,0:T(2,128)} %bitcast.23) | data formatting | bytes 65536
  2.3 0.8 %copy.15 = s32[64,4]{1,0:T(8,128)S(1)} copy(s32[64,4]{0,1:T(4,128)} %param.19) | data formatting | bytes 2048 | tf_op args[6]
  3.0 0.1 reshape.25.source_ref
  3.1 0.9 %pad.9.z_ref = f32[2,128,128]{2,1,0:T(8,128)S(1)} pad(f32[2,64,64]{2,1,0:T(8,128)} %param.25, f32[]{:T(128)} %constant.10.clone.1), padding=0_0x0_64x0_64 | pad | bytes 163844 | tf_op jit(solution)/shard_map/jit(_pad)/pad | solution.py:452
  4.0 0.0 copy-start
  4.0 2.2 %copy-done = bf16[64,16,32,32]{0,3,2,1:T(8,128)(2,1)S(1)} copy-done((bf16[64,16,32,32]{0,3,2,1:T(8,128)(2,1)S(1)}, bf16[64,16,32,32]{0,3,2,1:T(8,128)(2,1)}, u32[]{:S(2)}) %copy-start) | copy-done | bytes 2097176
  6.2 0.0 copy-start.1
  6.2 1.0 %copy-done.1 = bf16[64,32,128]{2,1,0:T(8,128)(2,1)S(1)} copy-done((bf16[64,32,128]{2,1,0:T(8,128)(2,1)S(1)}, bf16[64,32,128]{2,1,0:T(8,128)(2,1)}, u32[]{:S(2)}) %copy-start.1) | copy-done | bytes 524312
  7.2 0.0 copy-start.2
  7.2 1.0 %copy-done.2 = bf16[64,32,128]{2,1,0:T(8,128)(2,1)S(1)} copy-done((bf16[64,32,128]{2,1,0:T(8,128)(2,1)S(1)}, bf16[64,32,128]{2,1,0:T(8,128)(2,1)}, u32[]{:S(2)}) %copy-start.2) | copy-done | bytes 524312
  8.3 0.0 copy-start.3
  8.3 0.8 %copy-done.3 = s32[2,8192]{1,0:T(2,128)S(1)} copy-done((s32[2,8192]{1,0:T(2,128)S(1)}, s32[2,8192]{1,0:T(2,128)}, u32[]{:S(2)}) %copy-start.3) | copy-done | bytes 65560
  9.1 0.0 copy-start.4
  9.1 0.8 %copy-done.4 = s32[2,8192]{1,0:T(2,128)S(1)} copy-done((s32[2,8192]{1,0:T(2,128)S(1)}, s32[2,8192]{1,0:T(2,128)}, u32[]{:S(2)}) %copy-start.4) | copy-done | bytes 65560
  9.9 0.0 copy-start.5
  9.9 0.8 %copy-done.5 = f32[8192]{0:T(1024)S(1)} copy-done((f32[8192]{0:T(1024)S(1)}, f32[8192]{0:T(1024)}, u32[]{:S(2)}) %copy-start.5) | copy-done | bytes 32792
  10.7 0.0 copy-start.6
  10.7 0.7 %copy-done.6 = s32[16,128]{1,0:T(8,128)S(1)} copy-done((s32[16,128]{1,0:T(8,128)S(1)}, s32[16,128]{1,0:T(8,128)}, u32[]{:S(2)}) %copy-start.6) | copy-done | bytes 8216
  11.4 37.6 %shard_map.127 = f32[2,32,128]{2,1,0:T(8,128)S(1)} custom-call(s32[16,1,128]{2,1,0:T(1,128)S(1)} %bitcast.22, f32[2,32,128]{2,1,0:T(8,128)S(1)} %bitcast.18, s32[1,128]{1,0:T(1,128)S(1)} %subtract_bitcast_fusion.port_ref, s32[2,8192]{1,0:T(2,128)S(1)} %copy-done.3, s32[2,8192]{1,0:T(2,128)S(1)} %copy-done.4, bf16[2048,128]{1,0:T(8,128)(2,1)S(1)} %bitcast.17, ...), custom_call_target="tpu_custom_call" | custom-call | tf_op jit(solution)/shard_map/pallas_call | solution.py:459
  49.0 0.6 %copy.21 = f32[1,2,32,128]{3,1,2,0:T(2,128)} copy(f32[1,2,32,128]{3,2,1,0:T(8,128)S(1)} %bitcast.19) | data formatting | bytes 65536
Async XLA Ops:
  4.0 2.2 %copy-start = (bf16[64,16,32,32]{0,3,2,1:T(8,128)(2,1)S(1)}, bf16[64,16,32,32]{0,3,2,1:T(8,128)(2,1)}, u32[]{:S(2)}) copy-start(bf16[64,16,32,32]{0,3,2,1:T(8,128)(2,1)} %param.21) | copy-start | bytes 6291460
  6.2 1.0 %copy-start.1 = (bf16[64,32,128]{2,1,0:T(8,128)(2,1)S(1)}, bf16[64,32,128]{2,1,0:T(8,128)(2,1)}, u32[]{:S(2)}) copy-start(bf16[64,32,128]{2,1,0:T(8,128)(2,1)} %param.20) | copy-start | bytes 1572868
  7.2 1.0 %copy-start.2 = (bf16[64,32,128]{2,1,0:T(8,128)(2,1)S(1)}, bf16[64,32,128]{2,1,0:T(8,128)(2,1)}, u32[]{:S(2)}) copy-start(bf16[64,32,128]{2,1,0:T(8,128)(2,1)} %basis_out_ref.1) | copy-start | bytes 1572868
  8.3 0.8 %copy-start.3 = (s32[2,8192]{1,0:T(2,128)S(1)}, s32[2,8192]{1,0:T(2,128)}, u32[]{:S(2)}) copy-start(s32[2,8192]{1,0:T(2,128)} %entry_ref.1) | copy-start | bytes 196612
  9.1 0.8 %copy-start.4 = (s32[2,8192]{1,0:T(2,128)S(1)}, s32[2,8192]{1,0:T(2,128)}, u32[]{:S(2)}) copy-start(s32[2,8192]{1,0:T(2,128)} %sign_ref.1) | copy-start | bytes 196612
  9.9 0.8 %copy-start.5 = (f32[8192]{0:T(1024)S(1)}, f32[8192]{0:T(1024)}, u32[]{:S(2)}) copy-start(f32[8192]{0:T(1024)} %param.17) | copy-start | bytes 98308
  10.7 0.7 %copy-start.6 = (s32[16,128]{1,0:T(8,128)S(1)}, s32[16,128]{1,0:T(8,128)}, u32[]{:S(2)}) copy-start(s32[16,128]{1,0:T(8,128)} %param.16) | copy-start | bytes 24580
where the time goes:
time: 50.3 us; the launch traced here: 49.7 us
  Pallas kernels  37.6 us (75%)
  local copies, waits for them, and re-layouts  10.5 us (21%)
  other arithmetic  1.5 us (3%)
    pallas_call x1, Pallas kernels, per_device(): pl.pallas_call(functools.partial(whole_kernel, peers, rows, mesh_rows), o...  37.6 us
    unnamed x17, local copies, waits for them, and re-layouts  9.57 us

commit v1 on v0

v1 whole, which is shorter than its diff:
```python
import functools

import jax
import jax.numpy as jnp
from jax import lax
from jax.experimental import pallas as pl
from jax.experimental.pallas import tpu as pltpu
from jax.sharding import PartitionSpec as P

LANES = 128
GROUP = 8
LOOK_CHUNK = 2048
SUM_CHUNK = 2048
VMEM_LIMIT = 60 * 1024 * 1024
NT = (((1,), (1,)), ((), ()))
TN = (((0,), (0,)), ((), ()))


def greet(peers):
    me = lax.axis_index("clus")
    barrier = pltpu.get_barrier_semaphore()
    for step in range(1, peers):
        pl.semaphore_signal(
            barrier,
            inc=1,
            device_id={"clus": lax.rem(me + step, peers)},
            device_id_type=pl.DeviceIdType.MESH,
        )
    return lambda: pl.semaphore_wait(barrier, peers - 1)


def push(peers, phase, source_at, target_at, send_sem, recv_sem):
    me = lax.axis_index("clus")
    copies = []
    for step in range(1, peers):
        peer = lax.rem(me + step, peers)
        copy = pltpu.make_async_remote_copy(
            src_ref=source_at(step, peer),
            dst_ref=target_at(step, me),
            send_sem=send_sem.at[phase, step],
            recv_sem=recv_sem.at[phase, step],
            device_id={"clus": peer},
            device_id_type=pl.DeviceIdType.MESH,
        )
        copy.start()
        copies.append(copy)

    def arrive():
        for copy in copies:
            copy.wait_recv()

    def leave():
        for copy in copies:
            copy.wait_send()

    return arrive, leave


def one_hot(rows, index):
    match = lax.broadcasted_iota(jnp.int32, (rows, index.shape[1]), 0) == index
    return jnp.where(match, 1.0, 0.0).astype(jnp.bfloat16)


def pick(tables, low, row):
    sub = lax.broadcasted_iota(jnp.int32, (GROUP, LANES), 0)
    lanes = jnp.broadcast_to(low, (GROUP, LANES))
    gap = jnp.broadcast_to(row, (GROUP, LANES)) - sub
    total = [0.0, 0.0]
    for block in range(len(tables[0])):
        match = gap == block * GROUP
        for c in range(2):
            found = jnp.take_along_axis(
                tables[c][block], lanes, axis=1, mode="promise_in_bounds"
            )
            total[c] += jnp.where(match, found, 0.0)
    return total


def fold(value):
    return jnp.sum(value, axis=0, keepdims=True)


def blocks_of(table):
    return [table[start : start + GROUP] for start in range(0, table.shape[0], GROUP)]


def branch_flows(tables, first_row, add, entry_ref, sign_ref, flow_ref):
    groups = LOOK_CHUNK // (GROUP * LANES)

    @pl.loop(0, entry_ref.shape[1] // LOOK_CHUNK)
    def _(step):
        for group in range(groups):
            rows = [[], []]
            for j in range(GROUP):
                start = step * LOOK_CHUNK + (group * GROUP + j) * LANES
                columns = pl.ds(pl.multiple_of(start, LANES), LANES)
                total = [0.0, 0.0]
                for k in range(entry_ref.shape[0]):
                    entry = entry_ref[k : k + 1, columns]
                    orient = (2 * sign_ref[k : k + 1, columns] - 1).astype(jnp.float32)
                    found = pick(tables, entry & (LANES - 1), (entry >> 7) - first_row)
                    total = [total[c] + orient * found[c] for c in range(2)]
                for c in range(2):
                    rows[c].append(fold(total[c]))
            for c in range(2):
                start = (step * groups + group) * 2 * GROUP + c * GROUP
                place = pl.ds(pl.multiple_of(start, GROUP), GROUP)
                made = jnp.concatenate(rows[c], axis=0)
                flow_ref[place, :] = flow_ref[place, :] + made if add else made


def spread_sums(values, index, first_row, rows):
    low, row = index & (LANES - 1), (index >> 7) - first_row
    mask = lax.broadcasted_iota(jnp.int32, (rows, index.shape[1]), 0) == row
    high = [value.astype(jnp.bfloat16).astype(jnp.float32) for value in values]
    parts = high + [value - top for value, top in zip(values, high)]
    spread = [jnp.where(mask, part, 0.0).astype(jnp.bfloat16) for part in parts]
    return jnp.concatenate(spread, axis=0), one_hot(LANES, low)


def add_up(spread, hot):
    made = lax.dot_general(spread, hot, NT, preferred_element_type=jnp.float32)
    half = made.shape[0] // 2
    return made[:half] + made[half:]


def collect(entry_ref, sign_ref, voltage_ref, first_row, rows, o_ref):
    o_ref[...] = jnp.zeros_like(o_ref)
    groups = SUM_CHUNK // (GROUP * LANES)

    @pl.loop(0, entry_ref.shape[1] // SUM_CHUNK)
    def _(step):
        columns = pl.ds(pl.multiple_of(step * SUM_CHUNK, SUM_CHUNK), SUM_CHUNK)
        voltage = []
        for c in range(2):
            lines = []
            for group in range(groups):
                start = (step * groups + group) * 2 * GROUP + c * GROUP
                tile = voltage_ref[pl.ds(pl.multiple_of(start, GROUP), GROUP), :]
                lines += [tile[j : j + 1] for j in range(GROUP)]
            voltage.append(jnp.concatenate(lines, axis=1))
        made = []
        for k in range(entry_ref.shape[0]):
            orient = (2 * sign_ref[k : k + 1, columns] - 1).astype(jnp.float32)
            values = [orient * value for value in voltage]
            made.append(spread_sums(values, entry_ref[k : k + 1, columns], first_row, rows))
        o_ref[...] += add_up(
            jnp.concatenate([spread for spread, _ in made], axis=1),
            jnp.concatenate([hot for _, hot in made], axis=1),
        )


def far_coefficients(basis_ref, flow_ref, o_ref):
    flows = flow_ref[...].astype(jnp.bfloat16)
    count = flows.shape[0]
    tile_dev = count // 2
    rank = basis_ref.shape[0] // tile_dev
    lane = lax.broadcasted_iota(jnp.int32, (rank, count), 1)
    tile = (lane >> 4) * GROUP + (lane & (GROUP - 1))
    total = jnp.zeros((rank, count), jnp.float32)
    for start in range(0, tile_dev, GROUP):
        crossed = lax.dot_general(
            basis_ref[start * rank : (start + GROUP) * rank, :],
            flows,
            NT,
            preferred_element_type=jnp.float32,
        )
        for j in range(GROUP):
            total = jnp.where(tile == start + j, crossed[j * rank : (j + 1) * rank], total)
    o_ref[...] = total.astype(jnp.bfloat16)


def near_choice(source_ref, hot_ref):
    near_count, tile_dev = source_ref.shape
    count = 2 * tile_dev
    lane = lax.broadcasted_iota(jnp.int32, (tile_dev, count), 1)
    tile = (lane >> 4) * GROUP + (lane & (GROUP - 1))
    widen = lax.broadcasted_iota(jnp.int32, (tile_dev, count), 0) == tile
    source = jnp.dot(
        source_ref[...].astype(jnp.float32).astype(jnp.bfloat16),
        jnp.where(widen, 1.0, 0.0).astype(jnp.bfloat16),
        preferred_element_type=jnp.float32,
    ).astype(jnp.int32)
    part = lax.broadcasted_iota(jnp.int32, (near_count, count), 1) & GROUP
    place = (source >> 3) * 2 * GROUP + part + (source & (GROUP - 1))
    for k in range(near_count):
        hot = jnp.where(
            lax.broadcasted_iota(jnp.int32, (count, count), 0) == place[k : k + 1], 1.0, 0.0
        )
        hot_ref[k] = hot.T.astype(jnp.bfloat16)


def near_work(flow_ref, hot_ref, blocks_ref, picked_ref, near_ref):
    near_count = blocks_ref.shape[1]
    flows = flow_ref[...].astype(jnp.bfloat16)
    for k in range(near_count):
        picked_ref[:, k * LANES : (k + 1) * LANES] = jnp.dot(
            hot_ref[k], flows, preferred_element_type=jnp.float32
        ).astype(jnp.bfloat16)

    @pl.loop(0, blocks_ref.shape[0] // GROUP)
    def _(step):
        place = pl.ds(pl.multiple_of(step * 2 * GROUP, 2 * GROUP), 2 * GROUP)
        source = picked_ref[place, :]
        row = lax.broadcasted_iota(jnp.int32, (2 * GROUP, LANES), 0) & (GROUP - 1)
        total = jnp.zeros((2 * GROUP, LANES), jnp.float32)
        for j in range(GROUP):
            block = jnp.concatenate(
                [blocks_ref[step * GROUP + j, k] for k in range(near_count)], axis=1
            )
            made = lax.dot_general(source, block, NT, preferred_element_type=jnp.float32)
            total = jnp.where(row == j, made, total)
        near_ref[place, :] = total


def far_choice(peers, admissible_ref, hot_ref):
    far_count, tile_dev = admissible_ref.shape
    tiles = peers * tile_dev
    band = tiles // far_count
    first = lax.axis_index("clus") * tile_dev
    entry = lax.broadcasted_iota(jnp.int32, (far_count, tile_dev), 0)
    place = admissible_ref[...] - first - entry * band
    place = jnp.where(place < 0, place + tiles, place)
    place = jnp.where(place < 0, place + tiles, place)
    place = jnp.concatenate([place, place], axis=1)
    owner, tile = place // tile_dev, place % tile_dev
    lane = lax.broadcasted_iota(jnp.int32, (far_count, 2 * tile_dev), 1)
    part = jnp.where(lane < tile_dev, 0, GROUP)
    line = owner * 2 * tile_dev + (tile >> 3) * 2 * GROUP + part + (tile & (GROUP - 1))
    for k in range(far_count):
        hot_ref[k] = one_hot(hot_ref.shape[1], line[k : k + 1])


def far_mix(peers, coeff_ref, hot_ref, coupling_ref, picked_ref, mixed_ref):
    far_count, rank, _, tile_dev = coupling_ref.shape
    span = hot_ref.shape[1] // (2 * tile_dev)
    stride = peers // far_count
    for k in range(far_count):
        held = jnp.concatenate(
            [coeff_ref[(k * stride + j) % peers] for j in range(span)], axis=1
        )
        found = jnp.dot(held, hot_ref[k], preferred_element_type=jnp.float32)
        for c in range(2):
            picked_ref[c, k, :, :tile_dev] = found[:, c * tile_dev : (c + 1) * tile_dev]

    @pl.loop(0, rank)
    def _(r):
        total = [0.0, 0.0]
        for k in range(far_count):
            block = coupling_ref[k, r].astype(jnp.float32)
            total = [total[c] + block * picked_ref[c, k, :, :tile_dev] for c in range(2)]
        for c in range(2):
            mixed_ref[c, pl.ds(r, 1), :] = fold(total[c])


def voltages(mixed_ref, basis_ref, near_ref, flow_ref, resistance_ref, voltage_ref):
    rank, tile_dev = mixed_ref.shape[1:]
    width = GROUP * rank
    repeat = lax.broadcasted_iota(jnp.int32, (rank, width), 1) % rank
    repeat = jnp.where(
        lax.broadcasted_iota(jnp.int32, (rank, width), 0) == repeat, 1.0, 0.0
    ).astype(jnp.bfloat16)
    wide = [
        lax.dot_general(
            mixed_ref[c].T.astype(jnp.bfloat16), repeat, (((1,), (0,)), ((), ())),
            preferred_element_type=jnp.float32,
        )
        for c in range(2)
    ]
    mask = lax.broadcasted_iota(jnp.int32, (GROUP, width), 1) // rank
    mask = mask == lax.broadcasted_iota(jnp.int32, (GROUP, width), 0)
    for group in range(tile_dev // GROUP):
        own = slice(group * GROUP, (group + 1) * GROUP)
        mixed = jnp.concatenate([jnp.where(mask, wide[c][own], 0.0) for c in range(2)], axis=0)
        far = jnp.dot(
            mixed.astype(jnp.bfloat16),
            basis_ref[group * width : (group + 1) * width, :],
            preferred_element_type=jnp.float32,
        )
        place = slice(group * 2 * GROUP, (group + 1) * 2 * GROUP)
        reactive = near_ref[place, :] + far
        flow = flow_ref[place, :]
        resistance = resistance_ref[own, :]
        voltage_ref[place, :] = jnp.concatenate(
            [
                resistance * flow[:GROUP] - reactive[GROUP:],
                resistance * flow[GROUP:] + reactive[:GROUP],
            ],
            axis=0,
        )


def port_sums(current, z_ref):
    products = [
        lax.dot_general(
            current,
            z_ref[part],
            NT,
            precision=lax.Precision.HIGHEST,
            preferred_element_type=jnp.float32,
        )
        for part in range(2)
    ]
    return [products[0][0:1] - products[1][1:2], products[0][1:2] + products[1][0:1]]


def whole_kernel(
    peers,
    need_hbm,
    current_hbm,
    port_hbm,
    entry_hbm,
    sign_hbm,
    basis_in_hbm,
    source_hbm,
    blocks_hbm,
    admissible_hbm,
    coupling_hbm,
    basis_out_hbm,
    resistance_hbm,
    z_hbm,
    o_ref,
    need_ref,
    current_ref,
    port_ref,
    entry_ref,
    sign_ref,
    basis_in_ref,
    source_ref,
    blocks_ref,
    admissible_ref,
    coupling_ref,
    basis_out_ref,
    resistance_ref,
    z_ref,
    asked_ref,
    reply_ref,
    answer_ref,
    flow_ref,
    coeff_ref,
    near_hot_ref,
    near_picked_ref,
    near_ref,
    far_hot_ref,
    picked_ref,
    mixed_ref,
    voltage_ref,
    remote_ref,
    local_ref,
    slots_ref,
    arrived_ref,
    send_sem,
    recv_sem,
    load_sem,
):
    me = lax.axis_index("clus")
    met = greet(peers)
    pairs = [
        (need_hbm, need_ref),
        (current_hbm, current_ref),
        (entry_hbm, entry_ref),
        (sign_hbm, sign_ref),
        (port_hbm, port_ref),
        (source_hbm, source_ref),
        (admissible_hbm, admissible_ref),
        (basis_in_hbm, basis_in_ref),
        (blocks_hbm, blocks_ref),
        (coupling_hbm, coupling_ref),
        (basis_out_hbm, basis_out_ref),
        (resistance_hbm, resistance_ref),
        (z_hbm, z_ref),
    ]
    loads = [
        pltpu.make_async_copy(source, target, load_sem.at[i])
        for i, (source, target) in enumerate(pairs)
    ]
    for load in loads:
        load.start()
    (
        need_load,
        current_load,
        entry_load,
        sign_load,
        port_load,
        source_load,
        admissible_load,
        basis_in_load,
        blocks_load,
        coupling_load,
        basis_out_load,
        resistance_load,
        z_load,
    ) = loads
    sems = (send_sem, recv_sem)
    mesh_rows = current_ref.shape[0]
    ports = port_ref.shape[1]
    asked_ref[me] = jnp.full(asked_ref.shape[1:], -1, jnp.int32)
    need_load.wait()
    met()
    arrive, leave_need = push(
        peers,
        0,
        lambda step, peer: need_ref.at[peer],
        lambda step, own: asked_ref.at[own],
        *sems,
    )
    current_load.wait()
    entry_load.wait()
    sign_load.wait()
    own_tables = [blocks_of(current_ref[:, c, :]) for c in range(2)]
    branch_flows(own_tables, 0, False, entry_ref, sign_ref, flow_ref)
    port_load.wait()
    port = jnp.concatenate(
        [port_ref[...], jnp.full((1, LANES - ports), -1, jnp.int32)], axis=1
    ) - me * (mesh_rows * LANES)
    port_row = port >> 7
    held = pick(own_tables, port & (LANES - 1), port_row)
    port_current = [fold(held[c]) for c in range(2)]
    arrive()
    for p in range(peers):
        asked = asked_ref[p]
        found = pick(own_tables, asked & (LANES - 1), asked >> 7)
        reply_ref[p] = jnp.concatenate([fold(found[c]) for c in range(2)] + port_current, axis=0)
    arrive, leave_reply = push(
        peers,
        1,
        lambda step, peer: reply_ref.at[peer],
        lambda step, own: answer_ref.at[own],
        *sems,
    )
    answer_ref[me] = jnp.concatenate([jnp.zeros((2, LANES), jnp.float32)] + port_current, axis=0)
    source_load.wait()
    near_choice(source_ref, near_hot_ref)
    admissible_load.wait()
    far_choice(peers, admissible_ref, far_hot_ref)
    basis_in_load.wait()
    arrive()
    tables = [blocks_of(answer_ref[:, c, :]) for c in range(2)]
    branch_flows(tables, mesh_rows, True, entry_ref, sign_ref, flow_ref)
    far_coefficients(basis_in_ref, flow_ref, coeff_ref.at[0])
    arrive, leave_coeff = push(
        peers,
        2,
        lambda step, peer: coeff_ref.at[0],
        lambda step, own: coeff_ref.at[peers - step],
        *sems,
    )
    blocks_load.wait()
    near_work(flow_ref, near_hot_ref, blocks_ref, near_picked_ref, near_ref)
    coupling_load.wait()
    basis_out_load.wait()
    resistance_load.wait()
    arrive()
    far_mix(peers, coeff_ref, far_hot_ref, coupling_ref, picked_ref, mixed_ref)
    voltages(mixed_ref, basis_out_ref, near_ref, flow_ref, resistance_ref, voltage_ref)
    collect(entry_ref, sign_ref, voltage_ref, mesh_rows, peers, remote_ref)
    for c in range(2):
        slots_ref[:, c, :] = remote_ref[c * peers : (c + 1) * peers, :]
    arrive, leave_slots = push(
        peers,
        3,
        lambda step, peer: slots_ref.at[peer],
        lambda step, own: arrived_ref.at[own],
        *sems,
    )
    arrived_ref[me] = jnp.zeros(arrived_ref.shape[1:], jnp.float32)
    collect(entry_ref, sign_ref, voltage_ref, 0, mesh_rows, local_ref)
    z_load.wait()
    current = answer_ref[0]
    for p in range(1, peers):
        current = current + answer_ref[p]
    port_voltage = [
        jnp.concatenate([value, jnp.zeros((1, LANES - ports), jnp.float32)], axis=1)
        for value in port_sums(current[2:4, :ports], z_ref)
    ]
    asked = jnp.concatenate([asked_ref[p] for p in range(peers)] + [port], axis=1)
    for leave in (leave_need, leave_reply, leave_coeff):
        leave()
    arrive()
    values = [
        jnp.concatenate([arrived_ref[p, c : c + 1] for p in range(peers)] + [port_voltage[c]], axis=1)
        for c in range(2)
    ]
    total = local_ref[...] + add_up(*spread_sums(values, asked, 0, mesh_rows))
    for c in range(2):
        o_ref[:, c, :] = total[c * mesh_rows : (c + 1) * mesh_rows]
    leave_slots()


def per_device(
    mesh_current,
    branch_entry,
    branch_sign,
    need_slots,
    resistance,
    near_blocks,
    near_source,
    basis_in,
    coupling,
    basis_out,
    admissible,
    port_mesh,
    port_coupling,
):
    peers = lax.axis_size("clus")
    mesh_dev = mesh_current.shape[1]
    tile_dev, near_count, tile_width = near_blocks.shape[:3]
    rank = basis_in.shape[1]
    mesh_rows = mesh_dev // LANES
    far_count = admissible.shape[1]
    band = peers * tile_dev // far_count
    span = (band + tile_dev - 2) // tile_dev + 1
    operands = [
        need_slots[:, None, :],
        mesh_current.reshape(2, mesh_rows, LANES).transpose(1, 0, 2),
        port_mesh[None, :],
        branch_entry,
        branch_sign,
        basis_in.reshape(tile_dev * rank, tile_width),
        near_source.T,
        near_blocks,
        admissible.T,
        coupling.transpose(1, 2, 3, 0),
        basis_out.reshape(tile_dev * rank, tile_width),
        resistance.reshape(tile_dev, tile_width),
        port_coupling,
    ]
    f32, bf16 = jnp.float32, jnp.bfloat16
    tiles = pltpu.VMEM((2 * tile_dev, LANES), f32)
    message = pltpu.VMEM((peers, 2, LANES), f32)
    made = pl.pallas_call(
        functools.partial(whole_kernel, peers),
        out_shape=jax.ShapeDtypeStruct((mesh_rows, 2, LANES), f32),
        in_specs=[pl.BlockSpec(memory_space=pltpu.HBM)] * len(operands),
        out_specs=pl.BlockSpec(memory_space=pltpu.VMEM),
        scratch_shapes=[pltpu.VMEM(x.shape, x.dtype) for x in operands]
        + [
            pltpu.VMEM((peers, 1, LANES), jnp.int32),
            pltpu.VMEM((peers, 4, LANES), f32),
            pltpu.VMEM((peers, 4, LANES), f32),
            tiles,
            pltpu.VMEM((peers, rank, 2 * tile_dev), bf16),
            pltpu.VMEM((near_count, 2 * tile_dev, 2 * tile_dev), bf16),
            pltpu.VMEM((2 * tile_dev, near_count * LANES), bf16),
            tiles,
            pltpu.VMEM((far_count, span * 2 * tile_dev, 2 * tile_dev), bf16),
            pltpu.VMEM((2, far_count, rank, LANES), f32),
            pltpu.VMEM((2, rank, tile_dev), f32),
            tiles,
            pltpu.VMEM((2 * peers, LANES), f32),
            pltpu.VMEM((2 * mesh_rows, LANES), f32),
            message,
            message,
            pltpu.SemaphoreType.DMA((4, peers)),
            pltpu.SemaphoreType.DMA((4, peers)),
            pltpu.SemaphoreType.DMA((len(operands),)),
        ],
        compiler_params=pltpu.CompilerParams(
            collective_id=0, has_side_effects=True, vmem_limit_bytes=VMEM_LIMIT
        ),
    )(*operands)
    return made.transpose(1, 0, 2).reshape(2, mesh_dev)


def solution(mesh):
    both = ("groups", "clus")
    in_specs = (
        P(None, both),
        P(None, both),
        P(None, both),
        P(both, None),
        P(both),
        P(both, None, None, None),
        P(both, None),
        P(both, None, None),
        P(both, None, None, None),
        P(both, None, None),
        P(both, None),
        P("groups"),
        P(),
    )
    return jax.shard_map(
        per_device, mesh=mesh, in_specs=in_specs, out_specs=P(None, both), check_vma=False
    )
```

time: 50.3 us -> 33.4 us (0.66)
  local copies, waits for them, and re-layouts: 10.5 us -> 1.38 us
  Pallas kernels: 37.6 us -> 31.8 us
  other arithmetic: 1.5 us -> 0 us
    unnamed x17 -> x1, local copies, waits for them, and re-layouts: 9.57 us -> 1.38 us
    pallas_call x1, Pallas kernels: 37.6 us -> 31.8 us  [per_device(): pl.pallas_call(functools.partial(whole_kernel, peers), out_shape=jax.Shap...]
    pad x1 -> x0, local copies, waits for them, and re-layouts: 0.86 us -> none  [per_device(): jnp.pad(port_coupling, ((0, 0), (0, LANES - ports), (0, LANES - ports)))]
    concatenate x1 -> x0, other arithmetic: 0.85 us -> none  [per_device(): jnp.concatenate([admissible.T, admissible.T], axis=1).reshape(1, -1)]
    sub x1 -> x0, other arithmetic: 0.66 us -> none  [per_device(): jnp.pad(port_mesh, (0, LANES - ports), constant_values=-1)[None, :] - offset]
where the time goes in v1:
time: 33.4 us; the launch traced here: 33.2 us
  Pallas kernels  31.8 us (95%)
  local copies, waits for them, and re-layouts  1.38 us (4%)
    pallas_call x1, Pallas kernels, per_device(): pl.pallas_call(functools.partial(whole_kernel, peers), out_shape=jax.Shap...  31.8 us
    unnamed x1, local copies, waits for them, and re-layouts  1.38 us

profile of v1, /device:TPU:0, one launch (start us, length us, event | category | flops | bytes accessed | tf_op | source)
XLA Modules:
  0.0 33.2 jit_solution(6988209194502393734)
XLA Ops:
  0.0 31.8 %shard_map.127 = f32[32,2,128]{2,1,0:T(2,128)} custom-call(s32[16,1,128]{2,1,0:T(1,128)} %bitcast.20, f32[32,2,128]{2,1,0:T(2,128)} %bitcast.18, s32[1,64]{1,0:T(1,128)} %bitcast.23, s32[2,8192]{1,0:T(2,128)} %entry_hbm.1, s32[2,8192]{1,0:T(2,128)} %sign_hbm.1, bf16[2048,128]{1,0:T(8,128)(2,1)} %bitcast.15, s32[4,64]{1,0:T(4,128)} %bitcast.22, ...), custom_call_target="tpu_custom_call" | custom-call | tf_op jit(solution)/shard_map/pallas_call | solution.py:531
  31.8 1.4 %copy.15 = f32[2,4096]{1,0:T(2,128)} copy(f32[2,4096]{1,0:T(2,128)} %bitcast.17) | data formatting | bytes 65536

commit v2 on v1

--- a/solution.py
+++ b/solution.py
@@ -9,11 +9,12 @@
 
 LANES = 128
 GROUP = 8
-LOOK_CHUNK = 2048
-SUM_CHUNK = 2048
+LOCAL_CHUNK = 2048
+REMOTE_CHUNK = 8192
+HOT_CHUNK = 1024
+MIX_STEP = 4
 VMEM_LIMIT = 60 * 1024 * 1024
 NT = (((1,), (1,)), ((), ()))
-TN = (((0,), (0,)), ((), ()))
 
 
 def greet(peers):
@@ -84,15 +85,16 @@
     return [table[start : start + GROUP] for start in range(0, table.shape[0], GROUP)]
 
 
-def branch_flows(tables, first_row, add, entry_ref, sign_ref, flow_ref):
-    groups = LOOK_CHUNK // (GROUP * LANES)
-
-    @pl.loop(0, entry_ref.shape[1] // LOOK_CHUNK)
+def branch_flows(tables, first_row, add, chunk, entry_ref, sign_ref, flow_ref):
+    chunk = min(chunk, entry_ref.shape[1])
+    groups = chunk // (GROUP * LANES)
+
+    @pl.loop(0, entry_ref.shape[1] // chunk)
     def _(step):
         for group in range(groups):
             rows = [[], []]
             for j in range(GROUP):
-                start = step * LOOK_CHUNK + (group * GROUP + j) * LANES
+                start = step * chunk + (group * GROUP + j) * LANES
                 columns = pl.ds(pl.multiple_of(start, LANES), LANES)
                 total = [0.0, 0.0]
                 for k in range(entry_ref.shape[0]):
@@ -109,45 +111,64 @@
                 flow_ref[place, :] = flow_ref[place, :] + made if add else made
 
 
-def spread_sums(values, index, first_row, rows):
-    low, row = index & (LANES - 1), (index >> 7) - first_row
-    mask = lax.broadcasted_iota(jnp.int32, (rows, index.shape[1]), 0) == row
-    high = [value.astype(jnp.bfloat16).astype(jnp.float32) for value in values]
-    parts = high + [value - top for value, top in zip(values, high)]
-    spread = [jnp.where(mask, part, 0.0).astype(jnp.bfloat16) for part in parts]
-    return jnp.concatenate(spread, axis=0), one_hot(LANES, low)
-
-
-def add_up(spread, hot):
-    made = lax.dot_general(spread, hot, NT, preferred_element_type=jnp.float32)
-    half = made.shape[0] // 2
-    return made[:half] + made[half:]
-
-
-def collect(entry_ref, sign_ref, voltage_ref, first_row, rows, o_ref):
-    o_ref[...] = jnp.zeros_like(o_ref)
-    groups = SUM_CHUNK // (GROUP * LANES)
-
-    @pl.loop(0, entry_ref.shape[1] // SUM_CHUNK)
+def signed_hot(entry_ref, sign_ref, hot_ref):
+    @pl.loop(0, entry_ref.shape[1] // HOT_CHUNK)
     def _(step):
-        columns = pl.ds(pl.multiple_of(step * SUM_CHUNK, SUM_CHUNK), SUM_CHUNK)
-        voltage = []
-        for c in range(2):
-            lines = []
-            for group in range(groups):
-                start = (step * groups + group) * 2 * GROUP + c * GROUP
-                tile = voltage_ref[pl.ds(pl.multiple_of(start, GROUP), GROUP), :]
-                lines += [tile[j : j + 1] for j in range(GROUP)]
-            voltage.append(jnp.concatenate(lines, axis=1))
-        made = []
+        columns = pl.ds(pl.multiple_of(step * HOT_CHUNK, HOT_CHUNK), HOT_CHUNK)
         for k in range(entry_ref.shape[0]):
             orient = (2 * sign_ref[k : k + 1, columns] - 1).astype(jnp.float32)
-            values = [orient * value for value in voltage]
-            made.append(spread_sums(values, entry_ref[k : k + 1, columns], first_row, rows))
-        o_ref[...] += add_up(
-            jnp.concatenate([spread for spread, _ in made], axis=1),
-            jnp.concatenate([hot for _, hot in made], axis=1),
-        )
+            low = entry_ref[k : k + 1, columns] & (LANES - 1)
+            match = lax.broadcasted_iota(jnp.int32, (LANES, HOT_CHUNK), 0) == low
+            hot_ref[k, :, columns] = jnp.where(match, orient, 0.0).astype(jnp.bfloat16)
+
+
+def halves(value):
+    high = value.astype(jnp.bfloat16).astype(jnp.float32)
+    return high, value - high
+
+
+def spread_over(parts, row, rows):
+    mask = lax.broadcasted_iota(jnp.int32, (rows, row.shape[1]), 0) == row
+    return jnp.concatenate(
+        [jnp.where(mask, part, 0.0).astype(jnp.bfloat16) for part in parts], axis=0
+    )
+
+
+def add_up(hot, spread):
+    return lax.dot_general(hot, spread, NT, preferred_element_type=jnp.float32)
+
+
+def join(made):
+    turned = made.T
+    half = turned.shape[0] // 2
+    return turned[:half] + turned[half:]
+
+
+def collect(entry_ref, hot_ref, voltage_ref, first_row, rows, chunk):
+    count = entry_ref.shape[1]
+    chunk = min(chunk, count)
+    groups = chunk // (GROUP * LANES)
+
+    def body(step, total):
+        columns = pl.ds(pl.multiple_of(step * chunk, chunk), chunk)
+        parts = []
+        for part in range(2):
+            for c in range(2):
+                lines = []
+                for group in range(groups):
+                    start = (step * groups + group) * 2 * GROUP + c * GROUP
+                    tile = voltage_ref[part, pl.ds(pl.multiple_of(start, GROUP), GROUP), :]
+                    lines += [tile[j : j + 1] for j in range(GROUP)]
+                parts.append(jnp.concatenate(lines, axis=1))
+        for k in range(entry_ref.shape[0]):
+            row = (entry_ref[k : k + 1, columns] >> 7) - first_row
+            total += add_up(hot_ref[k, :, columns], spread_over(parts, row, rows))
+        return total
+
+    total = jnp.zeros((LANES, 4 * rows), jnp.float32)
+    if count == chunk:
+        return join(body(0, total))
+    return join(lax.fori_loop(0, count // chunk, body, total))
 
 
 def far_coefficients(basis_ref, flow_ref, o_ref):
@@ -231,42 +252,60 @@
         hot_ref[k] = one_hot(hot_ref.shape[1], line[k : k + 1])
 
 
-def far_mix(peers, coeff_ref, hot_ref, coupling_ref, picked_ref, mixed_ref):
-    far_count, rank, _, tile_dev = coupling_ref.shape
-    span = hot_ref.shape[1] // (2 * tile_dev)
+def pack_coupling(coupling_ref, packed_ref):
+    half = packed_ref.shape[1]
+
+    @pl.loop(0, packed_ref.shape[0])
+    def _(r):
+        for k in range(half):
+            pair = [coupling_ref[k, r], coupling_ref[k + half, r]]
+            packed_ref[r, k] = jnp.concatenate(pair, axis=1).astype(jnp.float32)
+
+
+def far_mix(peers, coeff_ref, hot_ref, packed_ref, picked_ref, mixed_ref):
+    rank, half = packed_ref.shape[:2]
+    far_count, span, count = hot_ref.shape
+    span //= count
     stride = peers // far_count
-    for k in range(far_count):
+    tile_dev = count // 2
+
+    def found(k):
         held = jnp.concatenate(
             [coeff_ref[(k * stride + j) % peers] for j in range(span)], axis=1
         )
-        found = jnp.dot(held, hot_ref[k], preferred_element_type=jnp.float32)
+        return jnp.dot(held, hot_ref[k], preferred_element_type=jnp.float32)
+
+    for k in range(half):
+        both = [found(k), found(k + half)]
         for c in range(2):
-            picked_ref[c, k, :, :tile_dev] = found[:, c * tile_dev : (c + 1) * tile_dev]
-
-    @pl.loop(0, rank)
-    def _(r):
-        total = [0.0, 0.0]
-        for k in range(far_count):
-            block = coupling_ref[k, r].astype(jnp.float32)
-            total = [total[c] + block * picked_ref[c, k, :, :tile_dev] for c in range(2)]
+            own = slice(c * tile_dev, (c + 1) * tile_dev)
+            picked_ref[c, k] = jnp.concatenate([one[:, own] for one in both], axis=1)
+
+    @pl.loop(0, rank // MIX_STEP)
+    def _(step):
+        total = [[0.0, 0.0] for _ in range(MIX_STEP)]
+        for k in range(half):
+            held = [picked_ref[c, k] for c in range(2)]
+            for j in range(MIX_STEP):
+                block = packed_ref[step * MIX_STEP + j, k]
+                total[j] = [total[j][c] + block * held[c] for c in range(2)]
         for c in range(2):
-            mixed_ref[c, pl.ds(r, 1), :] = fold(total[c])
+            for j in range(MIX_STEP):
+                mixed_ref[c, pl.ds(step * MIX_STEP + j, 1), :] = fold(total[j][c])
 
 
 def voltages(mixed_ref, basis_ref, near_ref, flow_ref, resistance_ref, voltage_ref):
-    rank, tile_dev = mixed_ref.shape[1:]
+    rank, tile_dev = mixed_ref.shape[1], mixed_ref.shape[2] // 2
     width = GROUP * rank
     repeat = lax.broadcasted_iota(jnp.int32, (rank, width), 1) % rank
     repeat = jnp.where(
         lax.broadcasted_iota(jnp.int32, (rank, width), 0) == repeat, 1.0, 0.0
     ).astype(jnp.bfloat16)
-    wide = [
-        lax.dot_general(
-            mixed_ref[c].T.astype(jnp.bfloat16), repeat, (((1,), (0,)), ((), ())),
-            preferred_element_type=jnp.float32,
-        )
-        for c in range(2)
-    ]
+    both = mixed_ref[...]
+    both = both[:, :, :tile_dev] + both[:, :, tile_dev:]
+    turned = jnp.concatenate([both[0], both[1]], axis=1).T.astype(jnp.bfloat16)
+    wide = jnp.dot(turned, repeat, preferred_element_type=jnp.float32)
+    wide = [wide[:tile_dev], wide[tile_dev:]]
     mask = lax.broadcasted_iota(jnp.int32, (GROUP, width), 1) // rank
     mask = mask == lax.broadcasted_iota(jnp.int32, (GROUP, width), 0)
     for group in range(tile_dev // GROUP):
@@ -281,13 +320,15 @@
         reactive = near_ref[place, :] + far
         flow = flow_ref[place, :]
         resistance = resistance_ref[own, :]
-        voltage_ref[place, :] = jnp.concatenate(
+        voltage = jnp.concatenate(
             [
                 resistance * flow[:GROUP] - reactive[GROUP:],
                 resistance * flow[GROUP:] + reactive[:GROUP],
             ],
             axis=0,
         )
+        for part, value in enumerate(halves(voltage)):
+            voltage_ref[part, place, :] = value
 
 
 def port_sums(current, z_ref):
@@ -342,11 +383,11 @@
     near_picked_ref,
     near_ref,
     far_hot_ref,
+    packed_ref,
+    sum_hot_ref,
     picked_ref,
     mixed_ref,
     voltage_ref,
-    remote_ref,
-    local_ref,
     slots_ref,
     arrived_ref,
     send_sem,
@@ -408,7 +449,7 @@
     entry_load.wait()
     sign_load.wait()
     own_tables = [blocks_of(current_ref[:, c, :]) for c in range(2)]
-    branch_flows(own_tables, 0, False, entry_ref, sign_ref, flow_ref)
+    branch_flows(own_tables, 0, False, LOCAL_CHUNK, entry_ref, sign_ref, flow_ref)
     port_load.wait()
     port = jnp.concatenate(
         [port_ref[...], jnp.full((1, LANES - ports), -1, jnp.int32)], axis=1
@@ -433,10 +474,13 @@
     near_choice(source_ref, near_hot_ref)
     admissible_load.wait()
     far_choice(peers, admissible_ref, far_hot_ref)
+    signed_hot(entry_ref, sign_ref, sum_hot_ref)
+    coupling_load.wait()
+    pack_coupling(coupling_ref, packed_ref)
     basis_in_load.wait()
     arrive()
     tables = [blocks_of(answer_ref[:, c, :]) for c in range(2)]
-    branch_flows(tables, mesh_rows, True, entry_ref, sign_ref, flow_ref)
+    branch_flows(tables, mesh_rows, True, REMOTE_CHUNK, entry_ref, sign_ref, flow_ref)
     far_coefficients(basis_in_ref, flow_ref, coeff_ref.at[0])
     arrive, leave_coeff = push(
         peers,
@@ -447,15 +491,14 @@
     )
     blocks_load.wait()
     near_work(flow_ref, near_hot_ref, blocks_ref, near_picked_ref, near_ref)
-    coupling_load.wait()
     basis_out_load.wait()
     resistance_load.wait()
     arrive()
-    far_mix(peers, coeff_ref, far_hot_ref, coupling_ref, picked_ref, mixed_ref)
+    far_mix(peers, coeff_ref, far_hot_ref, packed_ref, picked_ref, mixed_ref)
     voltages(mixed_ref, basis_out_ref, near_ref, flow_ref, resistance_ref, voltage_ref)
-    collect(entry_ref, sign_ref, voltage_ref, mesh_rows, peers, remote_ref)
+    remote = collect(entry_ref, sum_hot_ref, voltage_ref, mesh_rows, peers, REMOTE_CHUNK)
     for c in range(2):
-        slots_ref[:, c, :] = remote_ref[c * peers : (c + 1) * peers, :]
+        slots_ref[:, c, :] = remote[c * peers : (c + 1) * peers, :]
     arrive, leave_slots = push(
         peers,
         3,
@@ -464,7 +507,7 @@
         *sems,
     )
     arrived_ref[me] = jnp.zeros(arrived_ref.shape[1:], jnp.float32)
-    collect(entry_ref, sign_ref, voltage_ref, 0, mesh_rows, local_ref)
+    local = collect(entry_ref, sum_hot_ref, voltage_ref, 0, mesh_rows, LOCAL_CHUNK)
     z_load.wait()
     current = answer_ref[0]
     for p in range(1, peers):
@@ -481,9 +524,11 @@
         jnp.concatenate([arrived_ref[p, c : c + 1] for p in range(peers)] + [port_voltage[c]], axis=1)
         for c in range(2)
     ]
-    total = local_ref[...] + add_up(*spread_sums(values, asked, 0, mesh_rows))
+    high, low = zip(*[halves(value) for value in values])
+    spread = spread_over(high + low, asked >> 7, mesh_rows)
+    total = local + join(add_up(one_hot(LANES, asked & (LANES - 1)), spread))
     for c in range(2):
-        o_ref[:, c, :] = total[c * mesh_rows : (c + 1) * mesh_rows]
+        o_ref[c] = total[c * mesh_rows : (c + 1) * mesh_rows]
     leave_slots()
 
 
@@ -530,7 +575,7 @@
     message = pltpu.VMEM((peers, 2, LANES), f32)
     made = pl.pallas_call(
         functools.partial(whole_kernel, peers),
-        out_shape=jax.ShapeDtypeStruct((mesh_rows, 2, LANES), f32),
+        out_shape=jax.ShapeDtypeStruct((2, mesh_rows, LANES), f32),
         in_specs=[pl.BlockSpec(memory_space=pltpu.HBM)] * len(operands),
         out_specs=pl.BlockSpec(memory_space=pltpu.VMEM),
         scratch_shapes=[pltpu.VMEM(x.shape, x.dtype) for x in operands]
@@ -544,11 +589,11 @@
             pltpu.VMEM((2 * tile_dev, near_count * LANES), bf16),
             tiles,
             pltpu.VMEM((far_count, span * 2 * tile_dev, 2 * tile_dev), bf16),
-            pltpu.VMEM((2, far_count, rank, LANES), f32),
-            pltpu.VMEM((2, rank, tile_dev), f32),
-            tiles,
-            pltpu.VMEM((2 * peers, LANES), f32),
-            pltpu.VMEM((2 * mesh_rows, LANES), f32),
+            pltpu.VMEM((rank, far_count // 2, rank, 2 * tile_dev), f32),
+            pltpu.VMEM((branch_entry.shape[0], LANES, branch_entry.shape[1]), bf16),
+            pltpu.VMEM((2, far_count // 2, rank, 2 * tile_dev), f32),
+            pltpu.VMEM((2, rank, 2 * tile_dev), f32),
+            pltpu.VMEM((2, 2 * tile_dev, LANES), f32),
             message,
             message,
             pltpu.SemaphoreType.DMA((4, peers)),
@@ -559,7 +604,7 @@
             collective_id=0, has_side_effects=True, vmem_limit_bytes=VMEM_LIMIT
         ),
     )(*operands)
-    return made.transpose(1, 0, 2).reshape(2, mesh_dev)
+    return made.reshape(2, mesh_dev)
 
 
 def solution(mesh):

time: 33.4 us -> 31.6 us (0.946)
  Pallas kernels: 31.8 us -> 30 us
    pallas_call x1, Pallas kernels: 31.8 us -> 30 us  [per_device(): pl.pallas_call(functools.partial(whole_kernel, peers), out_shape=jax.Shap...]
where the time goes in v2:
time: 31.6 us; the launch traced here: 31.4 us
  Pallas kernels  30 us (95%)
  local copies, waits for them, and re-layouts  1.4 us (4%)
    pallas_call x1, Pallas kernels, per_device(): pl.pallas_call(functools.partial(whole_kernel, peers), out_shape=jax.Shap...  30 us
    unnamed x1, local copies, waits for them, and re-layouts  1.4 us

profile of v2, /device:TPU:0, one launch (start us, length us, event | category | flops | bytes accessed | tf_op | source)
XLA Modules:
  0.0 31.4 jit_solution(13555568740231469177)
XLA Ops:
  0.0 30.0 %shard_map.127 = f32[2,32,128]{2,1,0:T(8,128)} custom-call(s32[16,1,128]{2,1,0:T(1,128)} %bitcast.21, f32[32,2,128]{2,1,0:T(2,128)} %bitcast.19, s32[1,64]{1,0:T(1,128)} %bitcast.24, s32[2,8192]{1,0:T(2,128)} %entry_hbm.1, s32[2,8192]{1,0:T(2,128)} %sign_hbm.1, bf16[2048,128]{1,0:T(8,128)(2,1)} %bitcast.16, s32[4,64]{1,0:T(4,128)} %bitcast.23, ...), custom_call_target="tpu_custom_call" | custom-call | tf_op jit(solution)/shard_map/pallas_call | solution.py:576
  30.0 1.4 %copy.16 = f32[1,2,32,128]{3,1,2,0:T(2,128)} copy(f32[1,2,32,128]{3,2,1,0:T(8,128)} %bitcast.18) | data formatting | bytes 65536

commit v3 on v2

--- a/solution.py
+++ b/solution.py
@@ -13,7 +13,7 @@
 REMOTE_CHUNK = 8192
 HOT_CHUNK = 1024
 MIX_STEP = 4
-VMEM_LIMIT = 60 * 1024 * 1024
+VMEM_LIMIT = 44 * 1024 * 1024
 NT = (((1,), (1,)), ((), ()))
 
 
@@ -30,14 +30,26 @@
     return lambda: pl.semaphore_wait(barrier, peers - 1)
 
 
+def partner(peers, step):
+    me = lax.axis_index("clus")
+    if peers & (peers - 1):
+        return lax.rem(me + step, peers)
+    peer, bit = me, 1
+    while bit < peers:
+        if step & bit:
+            peer = peer + bit * (1 - 2 * lax.rem(lax.div(me, bit), 2))
+        bit *= 2
+    return peer
+
+
 def push(peers, phase, source_at, target_at, send_sem, recv_sem):
     me = lax.axis_index("clus")
     copies = []
-    for step in range(1, peers):
-        peer = lax.rem(me + step, peers)
+    for step in range(peers - 1, 0, -1):
+        peer = partner(peers, step)
         copy = pltpu.make_async_remote_copy(
-            src_ref=source_at(step, peer),
-            dst_ref=target_at(step, me),
+            src_ref=source_at(peer),
+            dst_ref=target_at(peer, me),
             send_sem=send_sem.at[phase, step],
             recv_sem=recv_sem.at[phase, step],
             device_id={"clus": peer},
@@ -262,7 +274,7 @@
             packed_ref[r, k] = jnp.concatenate(pair, axis=1).astype(jnp.float32)
 
 
-def far_mix(peers, coeff_ref, hot_ref, packed_ref, picked_ref, mixed_ref):
+def far_mix(peers, coeff_ref, hot_ref, packed_ref, picked_ref, partial_ref, mixed_ref):
     rank, half = packed_ref.shape[:2]
     far_count, span, count = hot_ref.shape
     span //= count
@@ -291,7 +303,14 @@
                 total[j] = [total[j][c] + block * held[c] for c in range(2)]
         for c in range(2):
             for j in range(MIX_STEP):
-                mixed_ref[c, pl.ds(step * MIX_STEP + j, 1), :] = fold(total[j][c])
+                blocks = blocks_of(total[j][c])
+                partial_ref[c, step * MIX_STEP + j] = functools.reduce(jnp.add, blocks)
+
+    for c in range(2):
+        for start in range(0, rank, GROUP):
+            mixed_ref[c, start : start + GROUP, :] = jnp.concatenate(
+                [fold(partial_ref[c, start + j]) for j in range(GROUP)], axis=0
+            )
 
 
 def voltages(mixed_ref, basis_ref, near_ref, flow_ref, resistance_ref, voltage_ref):
@@ -386,6 +405,7 @@
     packed_ref,
     sum_hot_ref,
     picked_ref,
+    partial_ref,
     mixed_ref,
     voltage_ref,
     slots_ref,
@@ -441,8 +461,8 @@
     arrive, leave_need = push(
         peers,
         0,
-        lambda step, peer: need_ref.at[peer],
-        lambda step, own: asked_ref.at[own],
+        lambda peer: need_ref.at[peer],
+        lambda peer, own: asked_ref.at[own],
         *sems,
     )
     current_load.wait()
@@ -465,8 +485,8 @@
     arrive, leave_reply = push(
         peers,
         1,
-        lambda step, peer: reply_ref.at[peer],
-        lambda step, own: answer_ref.at[own],
+        lambda peer: reply_ref.at[peer],
+        lambda peer, own: answer_ref.at[own],
         *sems,
     )
     answer_ref[me] = jnp.concatenate([jnp.zeros((2, LANES), jnp.float32)] + port_current, axis=0)
@@ -485,8 +505,8 @@
     arrive, leave_coeff = push(
         peers,
         2,
-        lambda step, peer: coeff_ref.at[0],
-        lambda step, own: coeff_ref.at[peers - step],
+        lambda peer: coeff_ref.at[0],
+        lambda peer, own: coeff_ref.at[lax.rem(own - peer + peers, peers)],
         *sems,
     )
     blocks_load.wait()
@@ -494,7 +514,7 @@
     basis_out_load.wait()
     resistance_load.wait()
     arrive()
-    far_mix(peers, coeff_ref, far_hot_ref, packed_ref, picked_ref, mixed_ref)
+    far_mix(peers, coeff_ref, far_hot_ref, packed_ref, picked_ref, partial_ref, mixed_ref)
     voltages(mixed_ref, basis_out_ref, near_ref, flow_ref, resistance_ref, voltage_ref)
     remote = collect(entry_ref, sum_hot_ref, voltage_ref, mesh_rows, peers, REMOTE_CHUNK)
     for c in range(2):
@@ -502,8 +522,8 @@
     arrive, leave_slots = push(
         peers,
         3,
-        lambda step, peer: slots_ref.at[peer],
-        lambda step, own: arrived_ref.at[own],
+        lambda peer: slots_ref.at[peer],
+        lambda peer, own: arrived_ref.at[own],
         *sems,
     )
     arrived_ref[me] = jnp.zeros(arrived_ref.shape[1:], jnp.float32)
@@ -517,6 +537,7 @@
         for value in port_sums(current[2:4, :ports], z_ref)
     ]
     asked = jnp.concatenate([asked_ref[p] for p in range(peers)] + [port], axis=1)
+    asked_hot = one_hot(LANES, asked & (LANES - 1))
     for leave in (leave_need, leave_reply, leave_coeff):
         leave()
     arrive()
@@ -526,7 +547,8 @@
     ]
     high, low = zip(*[halves(value) for value in values])
     spread = spread_over(high + low, asked >> 7, mesh_rows)
-    total = local + join(add_up(one_hot(LANES, asked & (LANES - 1)), spread))
+    made = add_up(spread, asked_hot)
+    total = local + made[: 2 * mesh_rows] + made[2 * mesh_rows :]
     for c in range(2):
         o_ref[c] = total[c * mesh_rows : (c + 1) * mesh_rows]
     leave_slots()
@@ -571,6 +593,7 @@
         port_coupling,
     ]
     f32, bf16 = jnp.float32, jnp.bfloat16
+    operands = [pltpu.with_memory_space_constraint(x, pltpu.HBM) for x in operands]
     tiles = pltpu.VMEM((2 * tile_dev, LANES), f32)
     message = pltpu.VMEM((peers, 2, LANES), f32)
     made = pl.pallas_call(
@@ -592,6 +615,7 @@
             pltpu.VMEM((rank, far_count // 2, rank, 2 * tile_dev), f32),
             pltpu.VMEM((branch_entry.shape[0], LANES, branch_entry.shape[1]), bf16),
             pltpu.VMEM((2, far_count // 2, rank, 2 * tile_dev), f32),
+            pltpu.VMEM((2, rank, GROUP, 2 * tile_dev), f32),
             pltpu.VMEM((2, rank, 2 * tile_dev), f32),
             pltpu.VMEM((2, 2 * tile_dev, LANES), f32),
             message,

time: 31.6 us -> 29.7 us (0.940)
  Pallas kernels: 30 us -> 28.9 us
  local copies, waits for them, and re-layouts: 1.4 us -> 0.64 us
    pallas_call x1, Pallas kernels: 30 us -> 28.9 us  [per_device(): pl.pallas_call(functools.partial(whole_kernel, peers), out_shape=jax.Shap...]
    unnamed x1, local copies, waits for them, and re-layouts: 1.4 us -> 0.64 us
where the time goes in v3:
time: 29.7 us; the launch traced here: 29.5 us
  Pallas kernels  28.9 us (97%)
  local copies, waits for them, and re-layouts  0.64 us (2%)
    pallas_call x1, Pallas kernels, per_device(): pl.pallas_call(functools.partial(whole_kernel, peers), out_shape=jax.Shap...  28.9 us
    unnamed x1, local copies, waits for them, and re-layouts  0.64 us

profile of v3, /device:TPU:0, one launch (start us, length us, event | category | flops | bytes accessed | tf_op | source)
XLA Modules:
  0.0 29.5 jit_solution(6056149551431791854)
XLA Ops:
  0.0 28.9 %shard_map.127 = f32[2,32,128]{2,1,0:T(8,128)S(1)} custom-call(s32[16,1,128]{2,1,0:T(1,128)} %bitcast.21, f32[32,2,128]{2,1,0:T(2,128)} %bitcast.19, s32[1,64]{1,0:T(1,128)} %bitcast.24, s32[2,8192]{1,0:T(2,128)} %entry_hbm.1, s32[2,8192]{1,0:T(2,128)} %sign_hbm.1, bf16[2048,128]{1,0:T(8,128)(2,1)} %bitcast.17, s32[4,64]{1,0:T(4,128)} %bitcast.23, ...), custom_call_target="tpu_custom_call" | custom-call | tf_op jit(solution)/shard_map/pallas_call | solution.py:599
  28.9 0.6 %copy.16 = f32[1,2,32,128]{3,1,2,0:T(2,128)} copy(f32[1,2,32,128]{3,2,1,0:T(8,128)S(1)} %bitcast.15) | data formatting | bytes 65536

commit v4 on v3

--- a/solution.py
+++ b/solution.py
@@ -32,8 +32,6 @@
 
 def partner(peers, step):
     me = lax.axis_index("clus")
-    if peers & (peers - 1):
-        return lax.rem(me + step, peers)
     peer, bit = me, 1
     while bit < peers:
         if step & bit:
@@ -42,10 +40,10 @@
     return peer
 
 
-def push(peers, phase, source_at, target_at, send_sem, recv_sem):
+def push(peers, phase, steps, source_at, target_at, send_sem, recv_sem):
     me = lax.axis_index("clus")
     copies = []
-    for step in range(peers - 1, 0, -1):
+    for step in reversed(steps):
         peer = partner(peers, step)
         copy = pltpu.make_async_remote_copy(
             src_ref=source_at(peer),
@@ -91,6 +89,27 @@
 
 def fold(value):
     return jnp.sum(value, axis=0, keepdims=True)
+
+
+def fold_rows(values):
+    line = lax.broadcasted_iota(jnp.int32, (GROUP, LANES), 0)
+    gap = GROUP // 2
+    while gap:
+        low = (line & gap) == 0
+
+        def swap(value):
+            down = pltpu.roll(value, gap, 0)
+            if 2 * gap == GROUP:
+                return down
+            return jnp.where(low, pltpu.roll(value, GROUP - gap, 0), down)
+
+        half = len(values) // 2
+        values = [
+            jnp.where(low, one, two) + swap(jnp.where(low, two, one))
+            for one, two in zip(values[:half], values[half:])
+        ]
+        gap //= 2
+    return values[0]
 
 
 def blocks_of(table):
@@ -115,11 +134,11 @@
                     found = pick(tables, entry & (LANES - 1), (entry >> 7) - first_row)
                     total = [total[c] + orient * found[c] for c in range(2)]
                 for c in range(2):
-                    rows[c].append(fold(total[c]))
+                    rows[c].append(total[c])
             for c in range(2):
                 start = (step * groups + group) * 2 * GROUP + c * GROUP
                 place = pl.ds(pl.multiple_of(start, GROUP), GROUP)
-                made = jnp.concatenate(rows[c], axis=0)
+                made = fold_rows(rows[c])
                 flow_ref[place, :] = flow_ref[place, :] + made if add else made
 
 
@@ -308,8 +327,8 @@
 
     for c in range(2):
         for start in range(0, rank, GROUP):
-            mixed_ref[c, start : start + GROUP, :] = jnp.concatenate(
-                [fold(partial_ref[c, start + j]) for j in range(GROUP)], axis=0
+            mixed_ref[c, start : start + GROUP, :] = fold_rows(
+                [partial_ref[c, start + j] for j in range(GROUP)]
             )
 
 
@@ -458,13 +477,21 @@
     asked_ref[me] = jnp.full(asked_ref.shape[1:], -1, jnp.int32)
     need_load.wait()
     met()
-    arrive, leave_need = push(
-        peers,
-        0,
-        lambda peer: need_ref.at[peer],
-        lambda peer, own: asked_ref.at[own],
-        *sems,
-    )
+    half = peers // 2
+    near_steps, far_steps = range(1, half), range(half, peers)
+    near_first = lax.div(me, half) * half
+    far_first = half - near_first
+    needs = [
+        push(
+            peers,
+            0,
+            steps,
+            lambda peer: need_ref.at[peer],
+            lambda peer, own: asked_ref.at[own],
+            *sems,
+        )
+        for steps in (far_steps, near_steps)
+    ]
     current_load.wait()
     entry_load.wait()
     sign_load.wait()
@@ -477,40 +504,59 @@
     port_row = port >> 7
     held = pick(own_tables, port & (LANES - 1), port_row)
     port_current = [fold(held[c]) for c in range(2)]
-    arrive()
-    for p in range(peers):
-        asked = asked_ref[p]
-        found = pick(own_tables, asked & (LANES - 1), asked >> 7)
-        reply_ref[p] = jnp.concatenate([fold(found[c]) for c in range(2)] + port_current, axis=0)
-    arrive, leave_reply = push(
-        peers,
-        1,
-        lambda peer: reply_ref.at[peer],
-        lambda peer, own: answer_ref.at[own],
-        *sems,
-    )
+    replies = []
+    for first, steps, (arrive, _) in (
+        (far_first, far_steps, needs[0]),
+        (near_first, near_steps, needs[1]),
+    ):
+        arrive()
+        for start in range(0, half, GROUP // 2):
+            found = []
+            for j in range(GROUP // 2):
+                asked = asked_ref[first + start + j]
+                found += pick(own_tables, asked & (LANES - 1), asked >> 7)
+            found = fold_rows(found)
+            for j in range(GROUP // 2):
+                reply_ref[first + start + j] = jnp.concatenate(
+                    [found[2 * j : 2 * j + 2]] + port_current, axis=0
+                )
+        replies.append(
+            push(
+                peers,
+                1,
+                steps,
+                lambda peer: reply_ref.at[peer],
+                lambda peer, own: answer_ref.at[own],
+                *sems,
+            )
+        )
     answer_ref[me] = jnp.concatenate([jnp.zeros((2, LANES), jnp.float32)] + port_current, axis=0)
     source_load.wait()
     near_choice(source_ref, near_hot_ref)
     admissible_load.wait()
     far_choice(peers, admissible_ref, far_hot_ref)
-    signed_hot(entry_ref, sign_ref, sum_hot_ref)
     coupling_load.wait()
     pack_coupling(coupling_ref, packed_ref)
     basis_in_load.wait()
-    arrive()
-    tables = [blocks_of(answer_ref[:, c, :]) for c in range(2)]
-    branch_flows(tables, mesh_rows, True, REMOTE_CHUNK, entry_ref, sign_ref, flow_ref)
+    for first, (arrive, _) in zip((near_first, far_first), reversed(replies)):
+        arrive()
+        own = pl.ds(first, half)
+        tables = [blocks_of(answer_ref[own, c, :]) for c in range(2)]
+        branch_flows(
+            tables, mesh_rows + first, True, REMOTE_CHUNK, entry_ref, sign_ref, flow_ref
+        )
     far_coefficients(basis_in_ref, flow_ref, coeff_ref.at[0])
     arrive, leave_coeff = push(
         peers,
         2,
+        range(1, peers),
         lambda peer: coeff_ref.at[0],
         lambda peer, own: coeff_ref.at[lax.rem(own - peer + peers, peers)],
         *sems,
     )
     blocks_load.wait()
     near_work(flow_ref, near_hot_ref, blocks_ref, near_picked_ref, near_ref)
+    signed_hot(entry_ref, sign_ref, sum_hot_ref)
     basis_out_load.wait()
     resistance_load.wait()
     arrive()
@@ -522,6 +568,7 @@
     arrive, leave_slots = push(
         peers,
         3,
+        range(1, peers),
         lambda peer: slots_ref.at[peer],
         lambda peer, own: arrived_ref.at[own],
         *sems,
@@ -538,8 +585,9 @@
     ]
     asked = jnp.concatenate([asked_ref[p] for p in range(peers)] + [port], axis=1)
     asked_hot = one_hot(LANES, asked & (LANES - 1))
-    for leave in (leave_need, leave_reply, leave_coeff):
+    for _, leave in needs + replies:
         leave()
+    leave_coeff()
     arrive()
     values = [
         jnp.concatenate([arrived_ref[p, c : c + 1] for p in range(peers)] + [port_voltage[c]], axis=1)

time: 29.7 us -> 29.3 us (0.987)
  Pallas kernels: 28.9 us -> 28.4 us
    pallas_call x1, Pallas kernels: 28.9 us -> 28.4 us  [per_device(): pl.pallas_call(functools.partial(whole_kernel, peers), out_shape=jax.Shap...]
where the time goes in v4:
time: 29.3 us; the launch traced here: 29.1 us
  Pallas kernels  28.4 us (97%)
  local copies, waits for them, and re-layouts  0.64 us (2%)
    pallas_call x1, Pallas kernels, per_device(): pl.pallas_call(functools.partial(whole_kernel, peers), out_shape=jax.Shap...  28.4 us
    unnamed x1, local copies, waits for them, and re-layouts  0.64 us

profile of v4, /device:TPU:0, one launch (start us, length us, event | category | flops | bytes accessed | tf_op | source)
XLA Modules:
  0.0 29.1 jit_solution(13453094371282228836)
XLA Ops:
  0.0 28.4 %shard_map.127 = f32[2,32,128]{2,1,0:T(8,128)S(1)} custom-call(s32[16,1,128]{2,1,0:T(1,128)} %bitcast.21, f32[32,2,128]{2,1,0:T(2,128)} %bitcast.19, s32[1,64]{1,0:T(1,128)} %bitcast.24, s32[2,8192]{1,0:T(2,128)} %entry_hbm.1, s32[2,8192]{1,0:T(2,128)} %sign_hbm.1, bf16[2048,128]{1,0:T(8,128)(2,1)} %bitcast.17, s32[4,64]{1,0:T(4,128)} %bitcast.23, ...), custom_call_target="tpu_custom_call" | custom-call | tf_op jit(solution)/shard_map/pallas_call | solution.py:647
  28.5 0.6 %copy.16 = f32[1,2,32,128]{3,1,2,0:T(2,128)} copy(f32[1,2,32,128]{3,2,1,0:T(8,128)S(1)} %bitcast.15) | data formatting | bytes 65536

commit v5 on v4

--- a/solution.py
+++ b/solution.py
@@ -12,22 +12,9 @@
 LOCAL_CHUNK = 2048
 REMOTE_CHUNK = 8192
 HOT_CHUNK = 1024
-MIX_STEP = 4
+MIX_STEP = 8
 VMEM_LIMIT = 44 * 1024 * 1024
 NT = (((1,), (1,)), ((), ()))
-
-
-def greet(peers):
-    me = lax.axis_index("clus")
-    barrier = pltpu.get_barrier_semaphore()
-    for step in range(1, peers):
-        pl.semaphore_signal(
-            barrier,
-            inc=1,
-            device_id={"clus": lax.rem(me + step, peers)},
-            device_id_type=pl.DeviceIdType.MESH,
-        )
-    return lambda: pl.semaphore_wait(barrier, peers - 1)
 
 
 def partner(peers, step):
@@ -38,6 +25,18 @@
             peer = peer + bit * (1 - 2 * lax.rem(lax.div(me, bit), 2))
         bit *= 2
     return peer
+
+
+def greet(peers):
+    barrier = pltpu.get_barrier_semaphore()
+    for step in reversed(range(1, peers)):
+        pl.semaphore_signal(
+            barrier,
+            inc=1,
+            device_id={"clus": partner(peers, step)},
+            device_id_type=pl.DeviceIdType.MESH,
+        )
+    return lambda: pl.semaphore_wait(barrier, peers - 1)
 
 
 def push(peers, phase, steps, source_at, target_at, send_sem, recv_sem):
@@ -332,7 +331,21 @@
             )
 
 
-def voltages(mixed_ref, basis_ref, near_ref, flow_ref, resistance_ref, voltage_ref):
+def base_voltages(near_ref, flow_ref, resistance_ref, base_ref):
+    for group in range(resistance_ref.shape[0] // GROUP):
+        place = slice(group * 2 * GROUP, (group + 1) * 2 * GROUP)
+        resistance = resistance_ref[group * GROUP : (group + 1) * GROUP, :]
+        reactive, flow = near_ref[place, :], flow_ref[place, :]
+        base_ref[place, :] = jnp.concatenate(
+            [
+                resistance * flow[:GROUP] - reactive[GROUP:],
+                resistance * flow[GROUP:] + reactive[:GROUP],
+            ],
+            axis=0,
+        )
+
+
+def voltages(mixed_ref, basis_ref, base_ref, voltage_ref):
     rank, tile_dev = mixed_ref.shape[1], mixed_ref.shape[2] // 2
     width = GROUP * rank
     repeat = lax.broadcasted_iota(jnp.int32, (rank, width), 1) % rank
@@ -355,15 +368,9 @@
             preferred_element_type=jnp.float32,
         )
         place = slice(group * 2 * GROUP, (group + 1) * 2 * GROUP)
-        reactive = near_ref[place, :] + far
-        flow = flow_ref[place, :]
-        resistance = resistance_ref[own, :]
+        base = base_ref[place, :]
         voltage = jnp.concatenate(
-            [
-                resistance * flow[:GROUP] - reactive[GROUP:],
-                resistance * flow[GROUP:] + reactive[:GROUP],
-            ],
-            axis=0,
+            [base[:GROUP] - far[GROUP:], base[GROUP:] + far[:GROUP]], axis=0
         )
         for part, value in enumerate(halves(voltage)):
             voltage_ref[part, place, :] = value
@@ -426,6 +433,7 @@
     picked_ref,
     partial_ref,
     mixed_ref,
+    base_ref,
     voltage_ref,
     slots_ref,
     arrived_ref,
@@ -559,20 +567,24 @@
     signed_hot(entry_ref, sign_ref, sum_hot_ref)
     basis_out_load.wait()
     resistance_load.wait()
+    base_voltages(near_ref, flow_ref, resistance_ref, base_ref)
     arrive()
     far_mix(peers, coeff_ref, far_hot_ref, packed_ref, picked_ref, partial_ref, mixed_ref)
-    voltages(mixed_ref, basis_out_ref, near_ref, flow_ref, resistance_ref, voltage_ref)
+    voltages(mixed_ref, basis_out_ref, base_ref, voltage_ref)
     remote = collect(entry_ref, sum_hot_ref, voltage_ref, mesh_rows, peers, REMOTE_CHUNK)
     for c in range(2):
         slots_ref[:, c, :] = remote[c * peers : (c + 1) * peers, :]
-    arrive, leave_slots = push(
-        peers,
-        3,
-        range(1, peers),
-        lambda peer: slots_ref.at[peer],
-        lambda peer, own: arrived_ref.at[own],
-        *sems,
-    )
+    slots = [
+        push(
+            peers,
+            3,
+            steps,
+            lambda peer: slots_ref.at[peer],
+            lambda peer, own: arrived_ref.at[own],
+            *sems,
+        )
+        for steps in (far_steps, near_steps)
+    ]
     arrived_ref[me] = jnp.zeros(arrived_ref.shape[1:], jnp.float32)
     local = collect(entry_ref, sum_hot_ref, voltage_ref, 0, mesh_rows, LOCAL_CHUNK)
     z_load.wait()
@@ -583,23 +595,28 @@
         jnp.concatenate([value, jnp.zeros((1, LANES - ports), jnp.float32)], axis=1)
         for value in port_sums(current[2:4, :ports], z_ref)
     ]
-    asked = jnp.concatenate([asked_ref[p] for p in range(peers)] + [port], axis=1)
-    asked_hot = one_hot(LANES, asked & (LANES - 1))
     for _, leave in needs + replies:
         leave()
     leave_coeff()
-    arrive()
-    values = [
-        jnp.concatenate([arrived_ref[p, c : c + 1] for p in range(peers)] + [port_voltage[c]], axis=1)
-        for c in range(2)
-    ]
-    high, low = zip(*[halves(value) for value in values])
-    spread = spread_over(high + low, asked >> 7, mesh_rows)
-    made = add_up(spread, asked_hot)
-    total = local + made[: 2 * mesh_rows] + made[2 * mesh_rows :]
+    total, extra, place = local, port_voltage, port
+    for first, (arrive, _) in zip((near_first, far_first), reversed(slots)):
+        index = [asked_ref[first + j] for j in range(half)]
+        index = jnp.concatenate(index + ([] if extra is None else [place]), axis=1)
+        asked_hot = one_hot(LANES, index & (LANES - 1))
+        arrive()
+        values = []
+        for c in range(2):
+            line = [arrived_ref[first + j, c : c + 1] for j in range(half)]
+            line += [] if extra is None else [extra[c]]
+            values.append(jnp.concatenate(line, axis=1))
+        high, low = zip(*[halves(value) for value in values])
+        made = add_up(spread_over(high + low, index >> 7, mesh_rows), asked_hot)
+        total = total + made[: 2 * mesh_rows] + made[2 * mesh_rows :]
+        extra = None
     for c in range(2):
         o_ref[c] = total[c * mesh_rows : (c + 1) * mesh_rows]
-    leave_slots()
+    for _, leave in slots:
+        leave()
 
 
 def per_device(
@@ -665,6 +682,7 @@
             pltpu.VMEM((2, far_count // 2, rank, 2 * tile_dev), f32),
             pltpu.VMEM((2, rank, GROUP, 2 * tile_dev), f32),
             pltpu.VMEM((2, rank, 2 * tile_dev), f32),
+            tiles,
             pltpu.VMEM((2, 2 * tile_dev, LANES), f32),
             message,
             message,

time: 29.3 us -> 29.2 us (level)
  no operation moved by 1% of the time
where the time goes in v5:
time: 29.2 us; the launch traced here: 29 us
  Pallas kernels  28.4 us (97%)
  local copies, waits for them, and re-layouts  0.64 us (2%)
    pallas_call x1, Pallas kernels, per_device(): pl.pallas_call(functools.partial(whole_kernel, peers), out_shape=jax.Shap...  28.4 us
    unnamed x1, local copies, waits for them, and re-layouts  0.64 us

profile of v5, /device:TPU:0, one launch (start us, length us, event | category | flops | bytes accessed | tf_op | source)
XLA Modules:
  0.0 29.0 jit_solution(13931069768465248755)
XLA Ops:
  0.0 28.4 %shard_map.127 = f32[2,32,128]{2,1,0:T(8,128)S(1)} custom-call(s32[16,1,128]{2,1,0:T(1,128)} %bitcast.21, f32[32,2,128]{2,1,0:T(2,128)} %bitcast.19, s32[1,64]{1,0:T(1,128)} %bitcast.24, s32[2,8192]{1,0:T(2,128)} %entry_hbm.1, s32[2,8192]{1,0:T(2,128)} %sign_hbm.1, bf16[2048,128]{1,0:T(8,128)(2,1)} %bitcast.17, s32[4,64]{1,0:T(4,128)} %bitcast.23, ...), custom_call_target="tpu_custom_call" | custom-call | tf_op jit(solution)/shard_map/pallas_call | solution.py:664
  28.4 0.6 %copy.16 = f32[1,2,32,128]{3,1,2,0:T(2,128)} copy(f32[1,2,32,128]{3,2,1,0:T(8,128)S(1)} %bitcast.15) | data formatting | bytes 65536
